TPU v7x, 128 devices: a whole 4x4x4 slice. The times are simulated.
128 devices in a mesh: blk: 16 (over z, y), cuts: 8 (over x, core).
Axes of the slice: x: 4, y: 4, z: 4, core: 2. Of those that a mesh axis runs over, the one named last changes fastest.
Arguments:
- integrals: bfloat16 [128, 4096, 3072], P('blk', None, 'cuts'), may hold values from -0.0234375 to 0.0234375
- amplitudes: bfloat16 [128, 128, 4096], P('blk', 'cuts'), may hold values from -6 to 6
- tile_index: int32 [128], replicated, may hold values from 0 to 127, as said below
- live_blocks: int32 [16], replicated, may hold values from 1 to 8, as said below
- pair_index: int32 [128, 2], replicated, may hold values from 0 to 159
- occ_energy: float32 [160], replicated, may hold values from -2 to -0.5
- ab_energy: float32 [3072], P('cuts'), may hold values from 0.5 to 4
Outputs:
- update: float32 [128, 3072], P(None, 'cuts')
Inputs may be any that keep to these rules, and one draw needn't show every extreme that they name: `tile_index`: A permutation of the stored tiles. Of the 8 slots of one group, at most 2 pair with tiles stored in one group (tile t is stored in group t // 8), and some group and store pair exactly 2 times. `live_blocks`: some group has all 8 slots live.
All inputs are finite; a program needn't handle non-finite values.
Results may differ from a plain program's by a relative error of at most 0.0003.
Values may be sent and summed in bfloat16 or wider, within the bound.
A program may use at most 192 MiB of HBM per device.

v0:
```python
import jax
import jax.numpy as jnp
from jax import lax
from jax.sharding import PartitionSpec as P

MOST = 2


def on_device(integrals, amplitudes, tile_index, live_blocks, pair_index, occ_energy, ab_energy):
    groups = lax.axis_size("blk")
    own_group = lax.axis_index("blk")
    per_group = integrals.shape[0]
    owner_grid = (tile_index // per_group).reshape(groups, per_group)
    slot_grid = (tile_index % per_group).reshape(groups, per_group)
    positions = jnp.arange(per_group, dtype=jnp.int32)
    live_grid = positions[None, :] < live_blocks[:, None]
    same_owner = owner_grid[:, :, None] == owner_grid[:, None, :]
    earlier = positions[None, :] < positions[:, None]
    rank_grid = jnp.sum(
        (same_owner & earlier[None, :, :] & live_grid[:, None, :]).astype(jnp.int32), axis=2
    )
    chosen = (owner_grid == own_group) & live_grid
    slot_numbers = jnp.arange(MOST, dtype=jnp.int32)
    picked = chosen[:, None, :] & (rank_grid[:, None, :] == slot_numbers[None, :, None])
    send_tile = jnp.sum(jnp.where(picked, slot_grid[:, None, :], 0), axis=2).reshape(-1)
    send_live = jnp.any(picked, axis=2).reshape(-1)
    my_owner = lax.dynamic_index_in_dim(owner_grid, own_group, 0, keepdims=False)
    my_rank = lax.dynamic_index_in_dim(rank_grid, own_group, 0, keepdims=False)
    receive_row = my_owner * MOST + my_rank
    whole_rows = lax.all_gather(amplitudes, "cuts", axis=1, tiled=True)
    selected = jnp.take(whole_rows, send_tile, axis=0)
    received = lax.all_to_all(
        jnp.where(send_live[:, None, None], selected, jnp.zeros_like(selected)),
        "blk",
        split_axis=0,
        concat_axis=0,
        tiled=True,
    )
    needed = jnp.take(received, receive_row, axis=0)
    live_count = lax.dynamic_index_in_dim(live_blocks, own_group, 0, keepdims=False)

    def accumulate(block_slot, running):
        tile_rows = lax.dynamic_index_in_dim(needed, block_slot, 0, keepdims=False)
        block_cols = lax.dynamic_index_in_dim(integrals, block_slot, 0, keepdims=False)
        return running + jnp.dot(tile_rows, block_cols, preferred_element_type=jnp.float32)

    partial_sum = lax.fori_loop(
        0, live_count, accumulate, jnp.zeros((needed.shape[1], integrals.shape[2]), jnp.float32)
    )
    orbitals = jnp.arange(occ_energy.shape[0], dtype=jnp.int32)
    first_energy = jnp.sum(
        jnp.where(pair_index[:, 0:1] == orbitals[None, :], occ_energy[None, :], 0.0), axis=1
    )
    second_energy = jnp.sum(
        jnp.where(pair_index[:, 1:2] == orbitals[None, :], occ_energy[None, :], 0.0), axis=1
    )
    denominator = first_energy[:, None] + second_energy[:, None] - ab_energy[None, :]
    ladder = lax.psum(partial_sum, "blk")
    return ladder / denominator


def solution(mesh):
    in_specs = (P("blk", None, "cuts"), P("blk", "cuts", None), P(), P(), P(), P(), P("cuts"))
    out_specs = P(None, "cuts")
    return jax.shard_map(
        on_device, mesh=mesh, in_specs=in_specs, out_specs=out_specs, check_vma=False
    )
```

profile of v0, /device:TPU:0, one launch (start us, length us, event | category | flops | bytes accessed | tf_op | source)
XLA Modules:
  0.0 739.5 jit_solution(16945729993768737613)
XLA Ops:
  6.5 0.7 all-gather.2.cloned.1.call-update
  7.3 0.7 and_select_fusion.1
  7.9 0.1 reshape.146
  8.1 0.7 compare_and_fusion
  8.8 0.1 copy.20
  8.9 0.1 copy.21
  9.1 0.1 convert_reduce_fusion
  9.3 0.1 copy.24
  9.4 0.1 reshape.148
  9.5 0.1 reshape.147
  9.6 0.1 copy.22
  9.7 0.1 broadcast_in_dim.84
  9.8 51.4 %all-gather.2.cloned.1.call-done = bf16[8,128,4096]{2,1,0:T(8,128)(2,1)} async-done(((bf16[8,16,4096]{2,1,0:T(8,128)(2,1)}), bf16[8,128,4096]{2,1,0:T(8,128)(2,1)}) %all-gather.2.cloned.1.call-update) | async-done | bytes 8388624 | tf_op jit(solution)/shard_map/all_gather | solution.py:30
  61.2 15.7 %gather_fusion = bf16[32,128,4096]{2,1,0:T(8,128)(2,1)} fusion(bf16[8,128,4096]{2,1,0:T(8,128)(2,1)} %all-gather.2.cloned.1.call-done, s32[1024]{0:T(1024)S(1)} %pad_clamp_fusion.1), kind=kCustom, calls=%fused_computation | custom fusion | bytes 67108992 | tf_op jit(solution)/shard_map/jit(_take)/gather | solution.py:31
  77.0 22.8 %select_select_fusion = bf16[32,128,4096]{2,1,0:T(8,128)(2,1)} fusion(bf16[32,128,4096]{2,1,0:T(8,128)(2,1)} %gather_fusion, pred[32]{0:T(512)(128)(4,1)S(1)} %compare_and_fusion.1, pred[32]{0:T(512)(128)(4,1)S(1)} %broadcast_in_dim.84), kind=kLoop, calls=%fused_computation.9 | loop fusion | flops 33554432 | bytes 67108928 | tf_op jit(solution)/shard_map/jit(_where)/select_n | solution.py:33
  99.8 7.2 all-to-all-start
  107.0 0.6 dynamic_slice.19
  107.6 0.2 add_reduce_fusion
  107.8 503.0 %all-to-all-done = bf16[32,128,4096]{2,1,0:T(8,128)(2,1)} async-done(((bf16[32,128,4096]{2,1,0:T(8,128)(2,1)}), bf16[32,128,4096]{2,1,0:T(8,128)(2,1)}, u32[]{:S(2)}, u32[]{:S(2)}) %all-to-all-start) | async-done | bytes 33554464 | tf_op jit(solution)/shard_map/all_to_all | solution.py:32
  610.8 6.2 gather_fusion.1
  617.0 7.5 %broadcast_select_fusion = bf16[8,128,4096]{2,1,0:T(8,128)(2,1)} fusion(bf16[8,128,4096]{2,1,0:T(8,128)(2,1)} %gather_fusion.1, pred[8]{0:T(512)(128)(4,1)S(1)} %compare_and_fusion.2), kind=kLoop, calls=%fused_computation.10 | loop fusion | flops 4194304 | bytes 16777224 | tf_op jit(solution)/shard_map/jit(_take)/select_n | solution.py:39
  624.5 21.8 %while.10 = (s32[]{:T(128)}, f32[128,384]{1,0:T(8,128)S(1)}, s32[]{:T(128)}, bf16[8,128,4096]{2,1,0:T(8,128)(2,1)}, bf16[8,4096,384]{2,1,0:T(8,128)(2,1)}, /*index=5*/s32[]{:T(128)}, s32[]{:T(128)}, s32[]{:T(128)}) while((s32[]{:T(128)}, f32[128,384]{1,0:T(8,128)S(1)}, s32[]{:T(128)}, bf16[8,128,4096]{2,1,0:T(8,128)(2,1)}, ...), condition=%wide.region_4.5_spmd, body=%wide.region_3.4_spmd.sunk | while | flops 402702336 | bytes 4588663 | solution.py:47
  625.1 2.9 fusion.18
  628.6 2.9 fusion.18
  632.2 2.9 fusion.18
  635.7 2.9 fusion.18
  639.2 2.9 fusion.18
  642.8 2.9 fusion.18
  646.3 0.7 copy-done
  647.0 0.1 select_reduce_fusion
  647.1 83.9 %all-reduce.2.cloned.1.call-done = f32[128,384]{1,0:T(8,128)} async-done(((f32[128,384]{1,0:T(8,128)}), f32[128,384]{1,0:T(8,128)}) %all-reduce.2.cloned.1.call-update) | async-done | bytes 196624 | tf_op jit(solution)/shard_map/psum | solution.py:58
  731.0 1.7 subtract_divide_fusion
  (27 shorter events, 0.4 us)
Async XLA Ops:
  6.5 54.7 %all-gather.2.cloned.1.call-start = ((), (), s32[]{:S(2)}) async-start(), calls=%async_computation.1 | async-start | bytes 9437184 | tf_op jit(solution)/shard_map/all_gather | solution.py:30
  99.8 7.2 copy-start.4
  99.8 511.0 %all-to-all-start = ((bf16[32,128,4096]{2,1,0:T(8,128)(2,1)}), bf16[32,128,4096]{2,1,0:T(8,128)(2,1)}, u32[]{:S(2)}, u32[]{:S(2)}) async-start(bf16[32,128,4096]{2,1,0:T(8,128)(2,1)} %select_select_fusion), calls=%async_computation | async-start | bytes 67108864 | tf_op jit(solution)/shard_map/all_to_all | solution.py:32
  107.0 624.0 %all-reduce.2.cloned.1.call-start = ((), (), s32[]{:S(2)}) async-start(), calls=%async_computation.2 | async-start | bytes 393216 | tf_op jit(solution)/shard_map/psum | solution.py:58
  617.0 30.0 %copy-start.3 = (s32[128,2]{0,1:T(2,128)S(1)}, s32[128,2]{0,1:T(2,128)}, u32[]{:S(2)}) copy-start(s32[128,2]{0,1:T(2,128)} %param.13) | copy-start | bytes 3076
  617.0 30.0 %copy-start.2 = (f32[160]{0:T(256)S(1)}, f32[160]{0:T(256)}, u32[]{:S(2)}) copy-start(f32[160]{0:T(256)} %param.14) | copy-start | bytes 1924
  617.0 114.0 %copy-start.1 = (f32[384]{0:T(512)S(1)}, f32[384]{0:T(512)}, u32[]{:S(2)}) copy-start(f32[384]{0:T(512)} %param.15) | copy-start | bytes 4612
  646.3 0.7 copy-start
Sparse Core Ops, SparseCore 0:
  9.0 52.1 all-gather.1
  647.1 83.8 all-reduce.1
where the time goes:
time: 740 us
  waiting for transfers between devices  639 us (86%)
  other arithmetic  33.9 us (5%)
  local copies, waits for them, and re-layouts  24.2 us (3%)
  matrix products  17.6 us (2%)
  between operations  13.5 us (2%)
    all_to_all x1, waiting for transfers between devices, on_device(): lax.all_to_all(jnp.where(send_live[:, None, None], selected, jnp.zeros_li...  503 us
    psum x1, waiting for transfers between devices, on_device(): ladder = lax.psum(partial_sum, 'blk')  83.9 us
    all_gather x1, waiting for transfers between devices, on_device(): whole_rows = lax.all_gather(amplitudes, 'cuts', axis=1, tiled=True)  51.4 us
    select_n x1, other arithmetic, on_device(): jnp.where(send_live[:, None, None], selected, jnp.zeros_like(selected))  22.8 us
    dot_general x6, matrix products, accumulate(): jnp.dot(tile_rows, block_cols, preferred_element_type=jnp.float32)  17.6 us
    gather x1, local copies, waits for them, and re-layouts, on_device(): selected = jnp.take(whole_rows, send_tile, axis=0)  15.7 us
  transfers between devices with their start and end apart: 3, of which 3 were waited for; matrix products, arithmetic and copies ran while one was open for 0% of the time, Pallas kernels for 0%

commit v1 on v0

--- a/solution.py
+++ b/solution.py
@@ -13,30 +13,20 @@
     owner_grid = (tile_index // per_group).reshape(groups, per_group)
     slot_grid = (tile_index % per_group).reshape(groups, per_group)
     positions = jnp.arange(per_group, dtype=jnp.int32)
-    live_grid = positions[None, :] < live_blocks[:, None]
     same_owner = owner_grid[:, :, None] == owner_grid[:, None, :]
     earlier = positions[None, :] < positions[:, None]
-    rank_grid = jnp.sum(
-        (same_owner & earlier[None, :, :] & live_grid[:, None, :]).astype(jnp.int32), axis=2
-    )
-    chosen = (owner_grid == own_group) & live_grid
+    rank_grid = jnp.sum((same_owner & earlier[None, :, :]).astype(jnp.int32), axis=2)
+    chosen = owner_grid == own_group
     slot_numbers = jnp.arange(MOST, dtype=jnp.int32)
     picked = chosen[:, None, :] & (rank_grid[:, None, :] == slot_numbers[None, :, None])
     send_tile = jnp.sum(jnp.where(picked, slot_grid[:, None, :], 0), axis=2).reshape(-1)
-    send_live = jnp.any(picked, axis=2).reshape(-1)
     my_owner = lax.dynamic_index_in_dim(owner_grid, own_group, 0, keepdims=False)
     my_rank = lax.dynamic_index_in_dim(rank_grid, own_group, 0, keepdims=False)
     receive_row = my_owner * MOST + my_rank
-    whole_rows = lax.all_gather(amplitudes, "cuts", axis=1, tiled=True)
-    selected = jnp.take(whole_rows, send_tile, axis=0)
-    received = lax.all_to_all(
-        jnp.where(send_live[:, None, None], selected, jnp.zeros_like(selected)),
-        "blk",
-        split_axis=0,
-        concat_axis=0,
-        tiled=True,
-    )
-    needed = jnp.take(received, receive_row, axis=0)
+    selected = jnp.take(amplitudes, send_tile, axis=0)
+    received = lax.all_to_all(selected, "blk", split_axis=0, concat_axis=0, tiled=True)
+    own_rows = jnp.take(received, receive_row, axis=0)
+    needed = lax.all_gather(own_rows, "cuts", axis=1, tiled=True)
     live_count = lax.dynamic_index_in_dim(live_blocks, own_group, 0, keepdims=False)
 
     def accumulate(block_slot, running):

time: 740 us -> 260 us (0.35)
  waiting for transfers between devices: 639 us -> 192 us
  other arithmetic: 33.9 us -> 8.78 us
  local copies, waits for them, and re-layouts: 24.2 us -> 7.62 us
    all_to_all x1, waiting for transfers between devices: 503 us -> 62.9 us  [on_device(): lax.all_to_all(selected, 'blk', split_axis=0, concat_axis=0, tiled=True)]
    select_n x4, other arithmetic: 30.3 us -> 5.86 us  [the longest x2 4.62 us: on_device(): selected = jnp.take(amplitudes, send_tile, axis=0)]
    gather x2, local copies, waits for them, and re-layouts: 22 us -> 5.58 us  [the longest x1 2.8 us: on_device(): own_rows = jnp.take(received, receive_row, axis=0)]
    dot_general x6 -> x8, matrix products: 17.6 us -> 23.5 us  [accumulate(): jnp.dot(tile_rows, block_cols, preferred_element_type=jnp.float32)]
where the time goes in v1:
time: 260 us
  waiting for transfers between devices  192 us (74%)
  matrix products  23.5 us (9%)
  between operations  13.6 us (5%)
  other arithmetic  8.78 us (3%)
  starting transfers between devices  8.27 us (3%)
  local copies, waits for them, and re-layouts  7.62 us (3%)
  loops' own time  6.3 us (2%)
    psum x1, waiting for transfers between devices, on_device(): ladder = lax.psum(partial_sum, 'blk')  81 us
    all_to_all x1, waiting for transfers between devices, on_device(): lax.all_to_all(selected, 'blk', split_axis=0, concat_axis=0, tiled=True)  62.9 us
    all_gather x1, waiting for transfers between devices, on_device(): needed = lax.all_gather(own_rows, 'cuts', axis=1, tiled=True)  48 us
    dot_general x8, matrix products, accumulate(): jnp.dot(tile_rows, block_cols, preferred_element_type=jnp.float32)  23.5 us
    all_to_all x1, starting transfers between devices, on_device(): lax.all_to_all(selected, 'blk', split_axis=0, concat_axis=0, tiled=True)  8.18 us
    another operation x1, loops' own time, on_device(): lax.fori_loop(0, live_count, accumulate, jnp.zeros((needed.shape[1], inte...  6.3 us
  transfers between devices with their start and end apart: 3, of which 3 were waited for; matrix products, arithmetic and copies ran while one was open for 0% of the time, Pallas kernels for 0%

profile of v1, /device:TPU:0, one launch (start us, length us, event | category | flops | bytes accessed | tf_op | source)
XLA Modules:
  0.0 260.0 jit_solution(2468017294147059530)
XLA Ops:
  6.5 0.8 and_select_fusion.1
  7.3 0.1 reshape.114
  7.4 0.1 copy.15
  7.5 0.1 copy.18
  7.5 0.1 broadcast_in_dim.68
  7.6 0.1 copy.19
  7.7 0.1 convert_reduce_fusion
  7.8 0.1 copy.20
  7.9 0.1 reshape.116
  8.0 0.1 reshape.115
  8.1 2.8 %gather_fusion = bf16[32,16,4096]{2,1,0:T(8,128)(2,1)} fusion(bf16[8,16,4096]{2,1,0:T(8,128)(2,1)S(1)} %copy-done, s32[1024]{0:T(1024)S(1)} %pad_clamp_fusion.1), kind=kCustom, calls=%fused_computation | custom fusion | bytes 8388736 | tf_op jit(solution)/shard_map/jit(_take)/gather | solution.py:26
  10.9 4.6 %broadcast_select_fusion = bf16[32,16,4096]{2,1,0:T(8,128)(2,1)} fusion(bf16[32,16,4096]{2,1,0:T(8,128)(2,1)} %gather_fusion, pred[32]{0:T(512)(128)(4,1)S(1)} %compare_and_fusion), kind=kLoop, calls=%fused_computation.9 | loop fusion | flops 2097152 | bytes 8388640 | tf_op jit(solution)/shard_map/jit(_take)/select_n | solution.py:26
  15.5 8.2 %all-to-all-start = ((bf16[32,16,4096]{2,1,0:T(8,128)(2,1)}), bf16[32,16,4096]{2,1,0:T(8,128)(2,1)}, u32[]{:S(2)}, u32[]{:S(2)}) async-start(bf16[32,16,4096]{2,1,0:T(8,128)(2,1)} %broadcast_select_fusion), calls=%async_computation | async-start | bytes 8388608 | tf_op jit(solution)/shard_map/all_to_all | solution.py:27
  23.8 0.2 add_reduce_fusion
  24.0 62.9 %all-to-all-done = bf16[32,16,4096]{2,1,0:T(8,128)(2,1)} async-done(((bf16[32,16,4096]{2,1,0:T(8,128)(2,1)}), bf16[32,16,4096]{2,1,0:T(8,128)(2,1)}, u32[]{:S(2)}, u32[]{:S(2)}) %all-to-all-start) | async-done | bytes 4194336 | tf_op jit(solution)/shard_map/all_to_all | solution.py:27
  87.0 2.8 %gather_fusion.1 = bf16[8,16,4096]{2,1,0:T(8,128)(2,1)S(1)} fusion(bf16[32,16,4096]{2,1,0:T(8,128)(2,1)} %all-to-all-done, s32[1024]{0:T(1024)S(1)} %pad_clamp_fusion), kind=kCustom, calls=%fused_computation.1 | custom fusion | bytes 2097184 | tf_op jit(solution)/shard_map/jit(_take)/gather | solution.py:28
  89.8 1.2 broadcast_select_fusion.1
  91.1 0.7 dynamic_slice.19
  91.8 48.0 %all-gather.2.cloned.1.call-done = bf16[8,128,4096]{2,1,0:T(8,128)(2,1)} async-done(((bf16[8,16,4096]{2,1,0:T(8,128)(2,1)}), bf16[8,128,4096]{2,1,0:T(8,128)(2,1)}) %all-gather.2.cloned.1.call-update) | async-done | bytes 8388624 | tf_op jit(solution)/shard_map/all_gather | solution.py:29
  139.8 29.8 %while.10 = (s32[]{:T(128)}, f32[128,384]{1,0:T(8,128)S(1)}, s32[]{:T(128)}, bf16[8,128,4096]{2,1,0:T(8,128)(2,1)}, bf16[8,4096,384]{2,1,0:T(8,128)(2,1)}, /*index=5*/s32[]{:T(128)}, s32[]{:T(128)}, s32[]{:T(128)}) while((s32[]{:T(128)}, f32[128,384]{1,0:T(8,128)S(1)}, s32[]{:T(128)}, bf16[8,128,4096]{2,1,0:T(8,128)(2,1)}, ...), condition=%wide.region_3.4_spmd, body=%wide.region_2.3_spmd.sunk | while | flops 402702336 | bytes 4588663 | solution.py:37
  140.5 2.9 %fusion.17 = f32[128,384]{1,0:T(8,128)S(1)} fusion(f32[128,384]{1,0:T(8,128)S(1)} %get-tuple-element.91, bf16[8,4096,384]{2,1,0:T(8,128)(2,1)} %get-tuple-element.102, s32[]{:T(128)S(6)} %select_n.108, bf16[8,128,4096]{2,1,0:T(8,128)(2,1)} %get-tuple-element.101), kind=kOutput, calls=%fused_computation.5.clone.1 | convolution fusion | flops 402702336 | bytes 4588544 | tf_op jit(solution)/shard_map/while/body/dot_general | solution.py:35
  144.2 2.9 %fusion.17 = f32[128,384]{1,0:T(8,128)S(1)} fusion(f32[128,384]{1,0:T(8,128)S(1)} %get-tuple-element.91, bf16[8,4096,384]{2,1,0:T(8,128)(2,1)} %get-tuple-element.102, s32[]{:T(128)S(6)} %select_n.108, bf16[8,128,4096]{2,1,0:T(8,128)(2,1)} %get-tuple-element.101), kind=kOutput, calls=%fused_computation.5.clone.1 | convolution fusion | flops 402702336 | bytes 4588544 | tf_op jit(solution)/shard_map/while/body/dot_general | solution.py:35
  147.8 2.9 %fusion.17 = f32[128,384]{1,0:T(8,128)S(1)} fusion(f32[128,384]{1,0:T(8,128)S(1)} %get-tuple-element.91, bf16[8,4096,384]{2,1,0:T(8,128)(2,1)} %get-tuple-element.102, s32[]{:T(128)S(6)} %select_n.108, bf16[8,128,4096]{2,1,0:T(8,128)(2,1)} %get-tuple-element.101), kind=kOutput, calls=%fused_computation.5.clone.1 | convolution fusion | flops 402702336 | bytes 4588544 | tf_op jit(solution)/shard_map/while/body/dot_general | solution.py:35
  151.5 2.9 %fusion.17 = f32[128,384]{1,0:T(8,128)S(1)} fusion(f32[128,384]{1,0:T(8,128)S(1)} %get-tuple-element.91, bf16[8,4096,384]{2,1,0:T(8,128)(2,1)} %get-tuple-element.102, s32[]{:T(128)S(6)} %select_n.108, bf16[8,128,4096]{2,1,0:T(8,128)(2,1)} %get-tuple-element.101), kind=kOutput, calls=%fused_computation.5.clone.1 | convolution fusion | flops 402702336 | bytes 4588544 | tf_op jit(solution)/shard_map/while/body/dot_general | solution.py:35
  155.1 2.9 %fusion.17 = f32[128,384]{1,0:T(8,128)S(1)} fusion(f32[128,384]{1,0:T(8,128)S(1)} %get-tuple-element.91, bf16[8,4096,384]{2,1,0:T(8,128)(2,1)} %get-tuple-element.102, s32[]{:T(128)S(6)} %select_n.108, bf16[8,128,4096]{2,1,0:T(8,128)(2,1)} %get-tuple-element.101), kind=kOutput, calls=%fused_computation.5.clone.1 | convolution fusion | flops 402702336 | bytes 4588544 | tf_op jit(solution)/shard_map/while/body/dot_general | solution.py:35
  158.7 2.9 %fusion.17 = f32[128,384]{1,0:T(8,128)S(1)} fusion(f32[128,384]{1,0:T(8,128)S(1)} %get-tuple-element.91, bf16[8,4096,384]{2,1,0:T(8,128)(2,1)} %get-tuple-element.102, s32[]{:T(128)S(6)} %select_n.108, bf16[8,128,4096]{2,1,0:T(8,128)(2,1)} %get-tuple-element.101), kind=kOutput, calls=%fused_computation.5.clone.1 | convolution fusion | flops 402702336 | bytes 4588544 | tf_op jit(solution)/shard_map/while/body/dot_general | solution.py:35
  162.4 2.9 %fusion.17 = f32[128,384]{1,0:T(8,128)S(1)} fusion(f32[128,384]{1,0:T(8,128)S(1)} %get-tuple-element.91, bf16[8,4096,384]{2,1,0:T(8,128)(2,1)} %get-tuple-element.102, s32[]{:T(128)S(6)} %select_n.108, bf16[8,128,4096]{2,1,0:T(8,128)(2,1)} %get-tuple-element.101), kind=kOutput, calls=%fused_computation.5.clone.1 | convolution fusion | flops 402702336 | bytes 4588544 | tf_op jit(solution)/shard_map/while/body/dot_general | solution.py:35
  166.0 2.9 %fusion.17 = f32[128,384]{1,0:T(8,128)S(1)} fusion(f32[128,384]{1,0:T(8,128)S(1)} %get-tuple-element.91, bf16[8,4096,384]{2,1,0:T(8,128)(2,1)} %get-tuple-element.102, s32[]{:T(128)S(6)} %select_n.108, bf16[8,128,4096]{2,1,0:T(8,128)(2,1)} %get-tuple-element.101), kind=kOutput, calls=%fused_computation.5.clone.1 | convolution fusion | flops 402702336 | bytes 4588544 | tf_op jit(solution)/shard_map/while/body/dot_general | solution.py:35
  169.7 0.7 copy-done.1
  170.4 0.1 select_reduce_fusion
  170.5 81.0 %all-reduce.2.cloned.1.call-done = f32[128,384]{1,0:T(8,128)} async-done(((f32[128,384]{1,0:T(8,128)}), f32[128,384]{1,0:T(8,128)}) %all-reduce.2.cloned.1.call-update) | async-done | bytes 196624 | tf_op jit(solution)/shard_map/psum | solution.py:48
  251.5 1.7 subtract_divide_fusion
  (27 shorter events, 0.2 us)
Async XLA Ops:
  6.5 1.6 copy-start
  15.5 71.4 %all-to-all-start = ((bf16[32,16,4096]{2,1,0:T(8,128)(2,1)}), bf16[32,16,4096]{2,1,0:T(8,128)(2,1)}, u32[]{:S(2)}, u32[]{:S(2)}) async-start(bf16[32,16,4096]{2,1,0:T(8,128)(2,1)} %broadcast_select_fusion), calls=%async_computation | async-start | bytes 8388608 | tf_op jit(solution)/shard_map/all_to_all | solution.py:27
  23.7 67.3 %copy-start.5 = (s32[16]{0:T(128)S(1)}, s32[16]{0:T(128)}, u32[]{:S(2)}) copy-start(s32[16]{0:T(128)} %param.12) | copy-start | bytes 196
  23.8 116.0 %all-gather.2.cloned.1.call-start = ((), (), s32[]{:S(2)}) async-start(), calls=%async_computation.1 | async-start | bytes 9437184 | tf_op jit(solution)/shard_map/all_gather | solution.py:29
  91.0 160.4 %all-reduce.2.cloned.1.call-start = ((), (), s32[]{:S(2)}) async-start(), calls=%async_computation.2 | async-start | bytes 393216 | tf_op jit(solution)/shard_map/psum | solution.py:48
  139.8 30.6 %copy-start.4 = (s32[128,2]{0,1:T(2,128)S(1)}, s32[128,2]{0,1:T(2,128)}, u32[]{:S(2)}) copy-start(s32[128,2]{0,1:T(2,128)} %param.13) | copy-start | bytes 3076
  139.8 30.6 %copy-start.3 = (f32[160]{0:T(256)S(1)}, f32[160]{0:T(256)}, u32[]{:S(2)}) copy-start(f32[160]{0:T(256)} %param.14) | copy-start | bytes 1924
  139.8 111.6 %copy-start.2 = (f32[384]{0:T(512)S(1)}, f32[384]{0:T(512)}, u32[]{:S(2)}) copy-start(f32[384]{0:T(512)} %param.15) | copy-start | bytes 4612
  169.7 0.7 copy-start.1
Sparse Core Ops, SparseCore 0:
  91.2 48.5 all-gather.1
  170.5 80.9 all-reduce.1

commit v2 on v1

v2 whole, which is shorter than its diff:
```python
import functools

import jax
import jax.numpy as jnp
from jax import lax
from jax.experimental import pallas as pl
from jax.experimental.pallas import tpu as pltpu
from jax.sharding import PartitionSpec as P

MOST = 2
WIDTHS = (512,) * 8
AHEAD = 2
MESH = pl.DeviceIdType.MESH


def moved(group, offset, sign):
    z = (group // 4 + sign * (offset // 4) + 4) % 4
    y = (group % 4 + sign * (offset % 4) + 4) % 4
    return z * 4 + y


def kernel(widths, *refs):
    parts = len(widths)
    starts = [sum(widths[:j]) for j in range(parts)]
    (send_pick, take_pick, live, pairs, occ, ab, integrals, amplitudes, out, tiles, total, sums, summed) = refs[:13]
    rest = refs[13:]
    blocks, leave, land, rows = (rest[i * parts:(i + 1) * parts] for i in range(4))
    (tile_sem, block_sem, leave_sem, land_sem, way_sem, from_low, from_high, from_low2, from_high2, from_twin,
     sum_send, sum_recv, out_send, out_recv, end_sem) = rest[4 * parts:]
    groups, cuts = lax.axis_size("blk"), lax.axis_size("cuts")
    group, cut = lax.axis_index("blk"), lax.axis_index("cuts")
    high, low, twin = (cut + 2) % cuts, (cut + cuts - 2) % cuts, cut + 1 - 2 * (cut % 2)
    far = (cut + 4) % cuts

    tile_copy = pltpu.make_async_copy(amplitudes, tiles, tile_sem)
    tile_copy.start()

    def block_copy(j):
        return pltpu.make_async_copy(integrals.at[:, pl.ds(starts[j], widths[j]), :], blocks[j], block_sem.at[j])

    for j in range(parts):
        block_copy(j).start()

    barrier = pltpu.get_barrier_semaphore()

    def greet(offset, carry):
        pl.semaphore_signal(barrier, inc=1, device_id={"blk": moved(group, offset, 1), "cuts": cut}, device_id_type=MESH)
        return carry

    lax.fori_loop(1, groups, greet, 0)
    for other in (high, low, twin):
        pl.semaphore_signal(barrier, inc=1, device_id={"blk": group, "cuts": other}, device_id_type=MESH)
    pl.semaphore_wait(barrier, groups - 1 + 3)
    tile_copy.wait()

    def spread(j):
        columns = pl.ds(starts[j], widths[j])
        for rank in range(MOST):
            land[j][rank] = tiles[send_pick[rank], :, columns]

        def one(offset, carry):
            for rank in range(MOST):
                leave[j][offset * MOST + rank] = tiles[send_pick[offset * MOST + rank], :, columns]
            place = pl.ds(offset * MOST, MOST)
            pltpu.make_async_remote_copy(
                src_ref=leave[j].at[place],
                dst_ref=land[j].at[place],
                send_sem=leave_sem.at[j],
                recv_sem=land_sem.at[j],
                device_id={"blk": moved(group, offset, 1), "cuts": cut},
                device_id_type=MESH,
            ).start()
            return carry

        lax.fori_loop(1, groups, one, 0)

    def along(j, owner, target, arrival, half=None):
        width = 8 * widths[j]
        columns = pl.ds(0, width) if half is None else pl.ds(half * (width // 2), width // 2)
        view = rows[j].at[pl.ds(pl.multiple_of(owner * 16, 16), 16), columns]
        return pltpu.make_async_remote_copy(
            src_ref=view,
            dst_ref=view,
            send_sem=way_sem.at[j],
            recv_sem=arrival.at[j],
            device_id={"blk": group, "cuts": target},
            device_id_type=MESH,
        )

    def wait_for(ref, semaphore):
        pltpu.make_async_copy(ref, ref, semaphore).wait()

    def piece(j, half=False):
        return rows[j].at[pl.ds(0, 16), pl.ds(0, 8 * widths[j] // (2 if half else 1))]

    def turn(j):
        wait_for(land[j].at[pl.ds(MOST, (groups - 1) * MOST)], land_sem.at[j])
        mine = pl.ds(pl.multiple_of(cut * 16, 16), 16)
        for block in range(8):
            tile = land[j][take_pick[block]]
            kept = jnp.where(live[block] > 0, tile, jnp.zeros_like(tile))
            rows[j][mine, pl.ds(block * widths[j], widths[j])] = kept
        along(j, cut, high, from_low).start()
        along(j, cut, low, from_high).start()
        along(j, cut, twin, from_twin).start()

    def relay(j):
        wait_for(piece(j), from_low.at[j])
        along(j, low, high, from_low2, 0).start()
        along(j, low, twin, from_twin).start()
        wait_for(piece(j), from_high.at[j])
        along(j, high, low, from_high2, 1).start()
        along(j, high, twin, from_twin).start()

    def finish(j):
        wait_for(piece(j, True), from_low2.at[j])
        along(j, far, twin, from_twin, 0).start()
        wait_for(piece(j, True), from_high2.at[j])
        along(j, far, twin, from_twin, 1).start()

    def multiply(j):
        wait_for(rows[j].at[pl.ds(0, 64)], from_twin.at[j])
        block_copy(j).wait()
        block = blocks[j][...].reshape(8 * widths[j], blocks[j].shape[2])
        product = jnp.dot(rows[j][...], block, preferred_element_type=jnp.float32)
        product = product.reshape(total.shape)
        if j == 0:
            total[...] = product
        else:
            total[...] += product

    for j in range(min(AHEAD, parts)):
        spread(j)
    for t in range(parts + 3):
        if t + AHEAD < parts:
            spread(t + AHEAD)
        if t < parts:
            turn(t)
        if 0 <= t - 1 < parts:
            relay(t - 1)
        if 0 <= t - 2 < parts:
            finish(t - 2)
        if 0 <= t - 3 < parts:
            multiply(t - 3)

    def scatter(offset, carry):
        target = moved(group, offset, 1)
        pltpu.make_async_remote_copy(
            src_ref=total.at[target],
            dst_ref=sums.at[offset],
            send_sem=sum_send,
            recv_sem=sum_recv,
            device_id={"blk": target, "cuts": cut},
            device_id_type=MESH,
        ).start()
        return carry

    lax.fori_loop(1, groups, scatter, 0)
    own_pairs = pairs[pl.ds(pl.multiple_of(group * 8, 8), 8), :]
    orbitals = lax.broadcasted_iota(jnp.int32, (8, occ.shape[1]), 1)
    energies = jnp.broadcast_to(occ[...], orbitals.shape)
    first = jnp.sum(jnp.where(own_pairs[:, 0:1] == orbitals, energies, 0.0), axis=1, keepdims=True)
    second = jnp.sum(jnp.where(own_pairs[:, 1:2] == orbitals, energies, 0.0), axis=1, keepdims=True)
    denominator = first + second - ab[...]
    wait_for(sums.at[pl.ds(1, groups - 1)], sum_recv)
    ladder = total[group]
    for offset in range(1, groups):
        ladder = ladder + sums[offset]
    summed[group] = ladder / denominator

    def share(offset, carry):
        pltpu.make_async_remote_copy(
            src_ref=summed.at[group],
            dst_ref=summed.at[group],
            send_sem=out_send,
            recv_sem=out_recv,
            device_id={"blk": moved(group, offset, 1), "cuts": cut},
            device_id_type=MESH,
        ).start()
        return carry

    lax.fori_loop(1, groups, share, 0)
    for j in range(parts):
        wait_for(leave[j].at[pl.ds(MOST, (groups - 1) * MOST)], leave_sem.at[j])
        wait_for(rows[j].at[pl.ds(0, 112)], way_sem.at[j])
    wait_for(sums.at[pl.ds(1, groups - 1)], sum_send)
    wait_for(sums.at[pl.ds(1, groups - 1)], out_recv)
    end = pltpu.make_async_copy(summed, out, end_sem)
    end.start()
    wait_for(sums.at[pl.ds(1, groups - 1)], out_send)
    end.wait()


def on_device(integrals, amplitudes, tile_index, live_blocks, pair_index, occ_energy, ab_energy):
    groups = lax.axis_size("blk")
    group = lax.axis_index("blk")
    per_group, depth, width = integrals.shape
    owner = tile_index // per_group
    slot = tile_index % per_group
    grid = owner.reshape(groups, per_group)
    positions = jnp.arange(per_group, dtype=jnp.int32)
    earlier = positions[None, :] < positions[:, None]
    rank = jnp.sum(((grid[:, :, None] == grid[:, None, :]) & earlier[None]).astype(jnp.int32), axis=2).reshape(-1)
    holder = jnp.arange(groups * per_group, dtype=jnp.int32) // per_group
    onward = moved(holder, group, -1)
    entry = onward * MOST + rank
    entries = jnp.arange(groups * MOST, dtype=jnp.int32)
    send_pick = jnp.sum(jnp.where((owner == group)[None] & (entry[None] == entries[:, None]), slot[None], 0), axis=1)
    backward = moved(group, owner, -1)
    take_pick = lax.dynamic_slice_in_dim(backward * MOST + rank, group * per_group, per_group)
    live = (positions < lax.dynamic_index_in_dim(live_blocks, group, 0, keepdims=False)).astype(jnp.int32)

    rows, parts = amplitudes.shape[1], len(WIDTHS)
    pairs = rows * lax.axis_size("cuts")
    part_rows = pairs // groups
    smem, vmem, hbm = (pl.BlockSpec(memory_space=space) for space in (pltpu.SMEM, pltpu.VMEM, pl.ANY))
    dma = pltpu.SemaphoreType.DMA
    scratch = [
        pltpu.VMEM(amplitudes.shape, jnp.bfloat16),
        pltpu.VMEM((groups, part_rows, width), jnp.float32),
        pltpu.VMEM((groups, part_rows, width), jnp.float32),
        pltpu.VMEM((groups, part_rows, width), jnp.float32),
    ]
    scratch += [pltpu.VMEM((per_group, each, width), jnp.bfloat16) for each in WIDTHS]
    scratch += [pltpu.VMEM((groups * MOST, rows, each), jnp.bfloat16) for each in WIDTHS] * 2
    scratch += [pltpu.VMEM((pairs, per_group * each), jnp.bfloat16) for each in WIDTHS]
    scratch += [dma] + [dma((parts,))] * 9 + [dma] * 5
    update = pl.pallas_call(
        functools.partial(kernel, WIDTHS),
        out_shape=jax.ShapeDtypeStruct((groups, part_rows, width), jnp.float32),
        in_specs=[smem, smem, smem, vmem, vmem, vmem, hbm, hbm],
        out_specs=hbm,
        scratch_shapes=scratch,
        compiler_params=pltpu.CompilerParams(collective_id=0, has_side_effects=True, vmem_limit_bytes=56 << 20),
        cost_estimate=pl.CostEstimate(flops=2 * pairs * per_group * depth * width, bytes_accessed=integrals.size * 2, transcendentals=0),
        name="ladder",
    )(send_pick, take_pick, live, pair_index, occ_energy[None], ab_energy[None], integrals, amplitudes)
    return update.reshape(pairs, width)


def solution(mesh):
    in_specs = (P("blk", None, "cuts"), P("blk", "cuts", None), P(), P(), P(), P(), P("cuts"))
    out_specs = P(None, "cuts")
    return jax.shard_map(
        on_device, mesh=mesh, in_specs=in_specs, out_specs=out_specs, check_vma=False
    )
```

time: 260 us -> 94.9 us (0.37)
  waiting for transfers between devices: 192 us -> 0 us
  Pallas kernels: 0 us -> 84.5 us
  matrix products: 23.5 us -> 0 us
  between operations: 13.6 us -> 0.02 us
  starting transfers between devices: 8.27 us -> 0 us
  loops' own time: 6.3 us -> 0 us
  other arithmetic: 8.78 us -> 3.3 us
    pallas_call x0 -> x1, Pallas kernels: none -> 84.5 us  [on_device(): pl.pallas_call(functools.partial(kernel, WIDTHS), out_shape=jax.ShapeDtyp...]
    psum x1 -> x0, waiting for transfers between devices: 81 us -> none  [on_device(): ladder = lax.psum(partial_sum, 'blk')]
    all_to_all x1 -> x0, waiting for transfers between devices: 62.9 us -> none  [on_device(): lax.all_to_all(selected, 'blk', split_axis=0, concat_axis=0, tiled=True)]
    all_gather x1 -> x0, waiting for transfers between devices: 48 us -> none  [on_device(): needed = lax.all_gather(own_rows, 'cuts', axis=1, tiled=True)]
    dot_general x8 -> x0, matrix products: 23.5 us -> none  [accumulate(): jnp.dot(tile_rows, block_cols, preferred_element_type=jnp.float32)]
    all_to_all x1 -> x0, starting transfers between devices: 8.18 us -> none  [on_device(): lax.all_to_all(selected, 'blk', split_axis=0, concat_axis=0, tiled=True)]
    select_n x5 -> x0, other arithmetic: 6.61 us -> none  [the longest x2 4.62 us: on_device(): selected = jnp.take(amplitudes, send_tile, axis=0)]
    another operation x1 -> x0, loops' own time: 6.3 us -> none  [on_device(): lax.fori_loop(0, live_count, accumulate, jnp.zeros((needed.shape[1], inte...]
  transfers between devices with their start and end apart: 3 -> 0, of which waited for: 3 -> 0; matrix products, arithmetic and copies ran while one was open for 0% -> 0% of each run, Pallas kernels for 0% -> 0%
where the time goes in v2:
time: 94.9 us; the launch traced here: 94.3 us
  Pallas kernels  84.5 us (89%)
  local copies, waits for them, and re-layouts  6.43 us (7%)
  other arithmetic  3.3 us (3%)
    pallas_call x1, Pallas kernels, on_device(): pl.pallas_call(functools.partial(kernel, WIDTHS), out_shape=jax.ShapeDtyp...  84.5 us
    unnamed x2, local copies, waits for them, and re-layouts  3.03 us

profile of v2, /device:TPU:0, one launch (start us, length us, event | category | flops | bytes accessed | tf_op | source)
XLA Modules:
  0.0 94.3 jit_solution(12772634448347848083)
XLA Ops:
  0.0 1.2 %dynamic_slice.8 = s32[1]{0:T(128)} dynamic-slice(s32[16]{0:T(128)} %param.10, s32[]{:T(128)S(6)} %select_n.106), dynamic_slice_sizes={1} | dynamic-slice | bytes 12 | tf_op jit(solution)/shard_map/jit(dynamic_index_in_dim)/dynamic_slice | solution.py:211
  1.2 1.2 %compare_convert_fusion.refs_2_ = s32[8]{0:T(128)} fusion(s32[]{:T(128)} %bitcast), kind=kLoop, calls=%fused_computation.13 | loop fusion | flops 16 | bytes 36 | tf_op jit(solution)/shard_map/convert_element_type | solution.py:211
  2.4 0.7 broadcast_compare_fusion
  3.1 1.3 %broadcast_in_dim.28.refs_5_ = f32[1,384]{1,0:T(1,128)} reshape(f32[384]{0:T(512)} %param.13) | data formatting | bytes 3072 | tf_op jit(solution)/shard_map/broadcast_in_dim | solution.py:237
  4.4 0.1 eq.47
  4.4 0.1 copy.10
  4.5 0.1 convert_reduce_fusion
  4.6 0.1 copy.12
  4.7 0.1 reshape.95
  4.8 0.7 multiply_add_fusion
  5.5 0.6 dynamic_slice.7.refs_1_
  6.1 0.7 select_reduce_fusion.refs_0_
  6.7 1.4 %copy.13.refs_3_ = s32[128,2]{1,0:T(8,128)} copy(s32[128,2]{0,1:T(2,128)} %param.11) | data formatting | bytes 2048 | tf_op args[4]
  8.1 84.5 %ladder.1 = f32[16,8,384]{2,1,0:T(8,128)} custom-call(s32[32]{0:T(128)} %select_reduce_fusion.refs_0_, s32[8]{0:T(128)} %dynamic_slice.7.refs_1_, s32[8]{0:T(128)} %compare_convert_fusion.refs_2_, s32[128,2]{1,0:T(8,128)} %copy.13.refs_3_, f32[1,160]{1,0:T(1,128)} %bitcast.4, f32[1,384]{1,0:T(1,128)} %broadcast_in_dim.28.refs_5_, ...), custom_call_target="tpu_custom_call" | custom-call | flops 3221225472 | bytes 25165824 | tf_op jit(solution)/shard_map/ladder/pallas_call | solution.py:228
  92.6 1.6 %copy.15 = f32[128,384]{1,0:T(8,128)} copy(f32[128,384]{1,0:T(8,128)} %bitcast.3) | data formatting | bytes 393216
  (1 shorter events, 0.0 us)

commit v3 on v2

v3 whole, which is shorter than its diff:
```python
import functools

import jax
import jax.numpy as jnp
from jax import lax
from jax.experimental import pallas as pl
from jax.experimental.pallas import tpu as pltpu
from jax.sharding import PartitionSpec as P

LANES = 128
PIECES = 4
SPREAD_AHEAD = 4
SORT_AHEAD = 2
MESH = pl.DeviceIdType.MESH


def moved(group, offset):
    z = (group // 4 + offset // 4) % 4
    y = (group % 4 + offset % 4) % 4
    return z * 4 + y


def kernel(parts, *refs):
    (tile_index, live_blocks, pairs, occ, ab, integrals, amplitudes, out) = refs[:8]
    (tiles, total, sums, summed) = refs[8:12]
    middle, leave = refs[12:14], refs[14:16]
    blocks, rows = refs[16:16 + parts], refs[16 + parts:16 + 2 * parts]
    (tile_sem, block_sem, spread_send, spread_recv, sort_send, sort_recv, way_sem, from_low, from_high, from_low2,
     from_high2, from_twin, sum_send, sum_recv, out_send, out_recv, end_sem) = refs[16 + 2 * parts:]
    groups, cuts = lax.axis_size("blk"), lax.axis_size("cuts")
    group, cut = lax.axis_index("blk"), lax.axis_index("cuts")
    high, low, twin = (cut + 2) % cuts, (cut + cuts - 2) % cuts, cut + 1 - 2 * (cut % 2)
    far = (cut + 4) % cuts
    width = integrals.shape[2]
    span = 8 * LANES

    tile_copy = pltpu.make_async_copy(amplitudes, tiles, tile_sem)
    tile_copy.start()

    barrier = pltpu.get_barrier_semaphore()

    def greet(offset, carry):
        pl.semaphore_signal(barrier, inc=1, device_id={"blk": moved(group, offset), "cuts": cut}, device_id_type=MESH)
        return carry

    lax.fori_loop(1, groups, greet, 0)
    for other in (high, low, twin):
        pl.semaphore_signal(barrier, inc=1, device_id={"blk": group, "cuts": other}, device_id_type=MESH)
    pl.semaphore_wait(barrier, groups - 1 + 3)
    tile_copy.wait()

    def wait_for(ref, semaphore):
        pltpu.make_async_copy(ref, ref, semaphore).wait()

    def block_copy(j, k):
        return pltpu.make_async_copy(
            integrals.at[:, pl.ds((j * PIECES + k) * LANES, LANES), :], blocks[j].at[pl.ds(k * 8, 8)], block_sem.at[j]
        )

    def spread(j):
        half = j // 4
        for k in range(PIECES):
            hub = k * 4 + (k + j) % 4
            source = tiles.at[:, :, pl.ds((j * PIECES + k) * LANES, LANES)]
            place = middle[half].at[pl.ds(pl.multiple_of(group * 8, 8), 8)]

            @pl.when(group == hub)
            def _():
                pltpu.make_async_copy(source, place, spread_recv.at[half]).start()

            @pl.when(group != hub)
            def _():
                pltpu.make_async_remote_copy(
                    src_ref=source,
                    dst_ref=place,
                    send_sem=spread_send.at[half],
                    recv_sem=spread_recv.at[half],
                    device_id={"blk": hub, "cuts": cut},
                    device_id_type=MESH,
                ).start()

    def sort(j):
        half = j // 4

        @pl.when(group % 4 == (group // 4 + j) % 4)
        def _():
            wait_for(middle[half], spread_recv.at[half])
            place = rows[j].at[pl.ds(pl.multiple_of(cut * 16, 16), 16), pl.ds(pl.multiple_of(group // 4 * span, span), span)]

            def pick(offset):
                target = moved(group, offset)
                live = live_blocks[target]
                for block in range(8):
                    tile = middle[half][tile_index[target * 8 + block]]
                    kept = jnp.where(live > block, tile, jnp.zeros_like(tile))
                    leave[half][offset, :, pl.ds(block * LANES, LANES)] = kept
                return target

            def one(offset, carry):
                target = pick(offset)
                pltpu.make_async_remote_copy(
                    src_ref=leave[half].at[offset],
                    dst_ref=place,
                    send_sem=sort_send.at[half],
                    recv_sem=sort_recv.at[j],
                    device_id={"blk": target, "cuts": cut},
                    device_id_type=MESH,
                ).start()
                return carry

            lax.fori_loop(1, groups, one, 0)
            pick(0)
            pltpu.make_async_copy(leave[half].at[0], place, sort_recv.at[j]).start()

    def along(j, owner, target, arrival, half=None):
        columns = pl.ds(0, PIECES * span) if half is None else pl.ds(half * (PIECES * span // 2), PIECES * span // 2)
        view = rows[j].at[pl.ds(pl.multiple_of(owner * 16, 16), 16), columns]
        return pltpu.make_async_remote_copy(
            src_ref=view,
            dst_ref=view,
            send_sem=way_sem.at[j],
            recv_sem=arrival.at[j],
            device_id={"blk": group, "cuts": target},
            device_id_type=MESH,
        )

    def piece(j, half=False):
        return rows[j].at[pl.ds(0, 16), pl.ds(0, PIECES * span // (2 if half else 1))]

    def turn(j):
        wait_for(piece(j), sort_recv.at[j])
        along(j, cut, high, from_low).start()
        along(j, cut, low, from_high).start()
        along(j, cut, twin, from_twin).start()
        for k in range(PIECES):
            block_copy(j, k).start()

    def relay(j):
        wait_for(piece(j), from_low.at[j])
        along(j, low, high, from_low2, 0).start()
        along(j, low, twin, from_twin).start()
        wait_for(piece(j), from_high.at[j])
        along(j, high, low, from_high2, 1).start()
        along(j, high, twin, from_twin).start()

    def finish(j):
        wait_for(piece(j, True), from_low2.at[j])
        along(j, far, twin, from_twin, 0).start()
        wait_for(piece(j, True), from_high2.at[j])
        along(j, far, twin, from_twin, 1).start()

    def multiply(j):
        wait_for(rows[j].at[pl.ds(0, 64)], from_twin.at[j])
        wait_for(blocks[j], block_sem.at[j])
        block = blocks[j][...].reshape(PIECES * span, width)
        product = jnp.dot(rows[j][...], block, preferred_element_type=jnp.float32)
        product = product.reshape(total.shape)
        if j == 0:
            total[...] = product
        else:
            total[...] += product

    for j in range(min(SPREAD_AHEAD, parts)):
        spread(j)
    for j in range(min(SORT_AHEAD, parts)):
        sort(j)
    for t in range(parts + 3):
        if t + SPREAD_AHEAD < parts:
            spread(t + SPREAD_AHEAD)
        if t + SORT_AHEAD < parts:
            sort(t + SORT_AHEAD)
        if t < parts:
            turn(t)
        if 0 <= t - 1 < parts:
            relay(t - 1)
        if 0 <= t - 2 < parts:
            finish(t - 2)
        if 0 <= t - 3 < parts:
            multiply(t - 3)

    def scatter(offset, carry):
        target = moved(group, offset)
        pltpu.make_async_remote_copy(
            src_ref=total.at[target],
            dst_ref=sums.at[offset],
            send_sem=sum_send,
            recv_sem=sum_recv,
            device_id={"blk": target, "cuts": cut},
            device_id_type=MESH,
        ).start()
        return carry

    lax.fori_loop(1, groups, scatter, 0)
    line = lax.broadcasted_iota(jnp.int32, (8, width), 0)
    energy = jnp.zeros((8, width), jnp.float32)
    for i in range(8):
        pair = group * 8 + i
        energy = jnp.where(line == i, occ[pairs[0, pair]] + occ[pairs[1, pair]], energy)
    denominator = energy - ab[...].reshape(1, width)
    wait_for(sums.at[pl.ds(1, groups - 1)], sum_recv)
    ladder = total[group]
    for offset in range(1, groups):
        ladder = ladder + sums[offset]
    summed[group] = ladder / denominator

    def share(offset, carry):
        pltpu.make_async_remote_copy(
            src_ref=summed.at[group],
            dst_ref=summed.at[group],
            send_sem=out_send,
            recv_sem=out_recv,
            device_id={"blk": moved(group, offset), "cuts": cut},
            device_id_type=MESH,
        ).start()
        return carry

    lax.fori_loop(1, groups, share, 0)
    for half in range(2):
        wait_for(middle[half].at[pl.ds(8, 120)], spread_send.at[half])
        wait_for(leave[half].at[pl.ds(1, groups - 1)], sort_send.at[half])
    for j in range(parts):
        wait_for(rows[j].at[pl.ds(0, 112)], way_sem.at[j])
    wait_for(sums.at[pl.ds(1, groups - 1)], sum_send)
    wait_for(sums.at[pl.ds(1, groups - 1)], out_recv)
    end = pltpu.make_async_copy(summed, out, end_sem)
    end.start()
    wait_for(sums.at[pl.ds(1, groups - 1)], out_send)
    end.wait()


def on_device(integrals, amplitudes, tile_index, live_blocks, pair_index, occ_energy, ab_energy):
    groups = lax.axis_size("blk")
    per_group, depth, width = integrals.shape
    rows = amplitudes.shape[1]
    pairs = rows * lax.axis_size("cuts")
    part_rows = pairs // groups
    parts = depth // (LANES * PIECES)
    smem, vmem, hbm = (pl.BlockSpec(memory_space=space) for space in (pltpu.SMEM, pltpu.VMEM, pl.ANY))
    dma = pltpu.SemaphoreType.DMA
    scratch = [pltpu.VMEM(amplitudes.shape, jnp.bfloat16)]
    scratch += [pltpu.VMEM((groups, part_rows, width), jnp.float32)] * 3
    scratch += [pltpu.VMEM((groups * per_group, rows, LANES), jnp.bfloat16)] * 2
    scratch += [pltpu.VMEM((groups, rows, per_group * LANES), jnp.bfloat16)] * 2
    scratch += [pltpu.VMEM((PIECES * per_group, LANES, width), jnp.bfloat16)] * parts
    scratch += [pltpu.VMEM((pairs, PIECES * per_group * LANES), jnp.bfloat16)] * parts
    scratch += [dma, dma((parts,)), dma((2,)), dma((2,)), dma((2,)), dma((parts,))] + [dma((parts,))] * 6 + [dma] * 5
    update = pl.pallas_call(
        functools.partial(kernel, parts),
        out_shape=jax.ShapeDtypeStruct((groups, part_rows, width), jnp.float32),
        in_specs=[smem, smem, smem, smem, vmem, hbm, hbm],
        out_specs=hbm,
        scratch_shapes=scratch,
        compiler_params=pltpu.CompilerParams(collective_id=0, has_side_effects=True, vmem_limit_bytes=56 << 20),
        cost_estimate=pl.CostEstimate(flops=2 * pairs * per_group * depth * width, bytes_accessed=integrals.size * 2, transcendentals=0),
        name="ladder",
    )(tile_index, live_blocks, pair_index.T, occ_energy, ab_energy, integrals, amplitudes)
    return update.reshape(pairs, width)


def solution(mesh):
    in_specs = (P("blk", None, "cuts"), P("blk", "cuts", None), P(), P(), P(), P(), P("cuts"))
    out_specs = P(None, "cuts")
    return jax.shard_map(
        on_device, mesh=mesh, in_specs=in_specs, out_specs=out_specs, check_vma=False
    )
```

time: 94.9 us -> 80.4 us (0.85)
  Pallas kernels: 84.5 us -> 77.9 us
  local copies, waits for them, and re-layouts: 6.43 us -> 1.62 us
  other arithmetic: 3.3 us -> 0 us
    pallas_call x1, Pallas kernels: 84.5 us -> 77.9 us  [on_device(): pl.pallas_call(functools.partial(kernel, parts), out_shape=jax.ShapeDtype...]
    dynamic_slice x2 -> x0, local copies, waits for them, and re-layouts: 1.83 us -> none  [the longest x1 1.24 us: on_device(): lax.dynamic_index_in_dim(live_blocks, group, 0, keepdims=False)]
    unnamed x2 -> x1, local copies, waits for them, and re-layouts: 3.03 us -> 1.62 us
    broadcast_in_dim x1 -> x0, local copies, waits for them, and re-layouts: 1.26 us -> none  [on_device(): ab_energy[None]]
    convert_element_type x1 -> x0, other arithmetic: 1.19 us -> none  [on_device(): (positions < lax.dynamic_index_in_dim(live_blocks, group, 0, keepdims=Fal...]
where the time goes in v3:
time: 80.4 us; the launch traced here: 79.5 us
  Pallas kernels  77.9 us (97%)
  local copies, waits for them, and re-layouts  1.62 us (2%)
    pallas_call x1, Pallas kernels, on_device(): pl.pallas_call(functools.partial(kernel, parts), out_shape=jax.ShapeDtype...  77.9 us
    unnamed x1, local copies, waits for them, and re-layouts  1.62 us

profile of v3, /device:TPU:0, one launch (start us, length us, event | category | flops | bytes accessed | tf_op | source)
XLA Modules:
  0.0 79.5 jit_solution(4978379271122758746)
XLA Ops:
  0.0 77.9 %ladder.1 = f32[16,8,384]{2,1,0:T(8,128)} custom-call(s32[128]{0:T(128)} %refs_0_.1, s32[16]{0:T(128)} %refs_1_.1, s32[2,128]{1,0:T(2,128)} %bitcast.3, f32[160]{0:T(256)} %refs_3_.1, f32[384]{0:T(512)} %refs_4_.1, bf16[8,4096,384]{2,1,0:T(8,128)(2,1)} %refs_5_.1, bf16[8,16,4096]{2,1,0:T(8,128)(2,1)} %refs_6_.1), custom_call_target="tpu_custom_call" | custom-call | flops 3221225472 | bytes 25165824 | tf_op jit(solution)/shard_map/ladder/pallas_call | solution.py:247
  77.9 1.6 %copy.9 = f32[128,384]{1,0:T(8,128)} copy(f32[128,384]{1,0:T(8,128)} %bitcast.2) | data formatting | bytes 393216

commit v4 on v3

v4 whole, which is shorter than its diff:
```python
import functools

import jax
import jax.numpy as jnp
from jax import lax
from jax.experimental import pallas as pl
from jax.experimental.pallas import tpu as pltpu
from jax.sharding import PartitionSpec as P

LANES = 128
QUARTERS = 4
HUBS = 8
CHUNKS = tuple((quarter, first, 4) for quarter in range(QUARTERS) for first in range(0, 8, 4))
SORT_AHEAD = 2
STRIDE = 5
MESH = pl.DeviceIdType.MESH


def moved(group, offset):
    return ((group + (offset & 12)) & 12) | ((group + offset) & 3)


def kernel(chunks, *refs):
    parts = len(chunks)
    (tile_index, live_blocks, pairs, occ, ab, integrals, amplitudes, out) = refs[:8]
    (tiles, total, sums, mine) = refs[8:12]
    middle, leave = refs[12:14], refs[14:16]
    blocks, rows = refs[16:16 + parts], refs[16 + parts:16 + 2 * parts]
    (tile_sem, block_sem, spread_send, spread_recv, sort_send, sort_recv, way_sem, from_low, from_high, from_low2,
     from_high2, from_twin, sum_send, sum_recv, out_send, out_recv, end_sem) = refs[16 + 2 * parts:]
    groups, cuts = lax.axis_size("blk"), lax.axis_size("cuts")
    group, cut = lax.axis_index("blk"), lax.axis_index("cuts")
    high, low, twin = (cut + 2) & (cuts - 1), (cut - 2) & (cuts - 1), cut ^ 1
    far = cut ^ 4
    width = integrals.shape[2]
    span = HUBS * LANES

    tile_copy = pltpu.make_async_copy(amplitudes, tiles, tile_sem)
    tile_copy.start()

    barrier = pltpu.get_barrier_semaphore()

    def greet(offset, carry):
        pl.semaphore_signal(barrier, inc=1, device_id={"blk": moved(group, offset), "cuts": cut}, device_id_type=MESH)
        return carry

    lax.fori_loop(1, groups, greet, 0)
    for other in (high, low, twin):
        pl.semaphore_signal(barrier, inc=1, device_id={"blk": group, "cuts": other}, device_id_type=MESH)
    pl.semaphore_wait(barrier, groups - 1 + 3)
    tile_copy.wait()

    def wait_for(ref, semaphore):
        pltpu.make_async_copy(ref, ref, semaphore).wait()

    def block_copy(j):
        quarter, first, count = chunks[j]
        return pltpu.make_async_copy(
            integrals.at[pl.ds(first, count), pl.ds(quarter * span, span), :], blocks[j], block_sem.at[j]
        )

    def is_hub(quarter):
        return (((group >> 2) + group) & 1) == ((cut + quarter) & 1)

    def spread(quarter):
        half = quarter // 2
        place = middle[half].at[pl.ds(pl.multiple_of(group * 8, 8), 8)]

        def source(index):
            return tiles.at[:, :, pl.ds(pl.multiple_of(quarter * span + index * LANES, LANES), LANES)]

        def remote(step):
            index = ((group >> 1) + step) & (HUBS - 1)
            hub = (index << 1) | (((index >> 1) + cut + quarter) & 1)
            return pltpu.make_async_remote_copy(
                src_ref=source(index),
                dst_ref=place,
                send_sem=spread_send.at[half],
                recv_sem=spread_recv.at[half],
                device_id={"blk": hub, "cuts": cut},
                device_id_type=MESH,
            )

        def one(step, carry):
            remote(step).start()
            return carry

        lax.fori_loop(1, HUBS, one, 0)

        @pl.when(is_hub(quarter))
        def _():
            pltpu.make_async_copy(source(group >> 1), place, spread_recv.at[half]).start()

        @pl.when(jnp.logical_not(is_hub(quarter)))
        def _():
            remote(0).start()

    def sort(j):
        quarter, first, count = chunks[j]
        half = quarter // 2

        @pl.when(is_hub(quarter))
        def _():
            if first == 0:
                wait_for(middle[half], spread_recv.at[half])
            column = pl.multiple_of((group >> 1) * LANES, LANES)
            place = rows[j].at[pl.ds(0, count), pl.ds(pl.multiple_of(cut * 16, 16), 16), pl.ds(column, LANES)]

            def pick(offset):
                target = moved(group, offset)
                live = live_blocks[target]
                for block in range(first, first + count):
                    tile = middle[half][tile_index[target * 8 + block]]
                    leave[half][offset, block] = jnp.where(live > block, tile, jnp.zeros_like(tile))
                return target

            def one(step, carry):
                offset = (step * STRIDE) & 15
                target = pick(offset)
                pltpu.make_async_remote_copy(
                    src_ref=leave[half].at[offset, pl.ds(first, count)],
                    dst_ref=place,
                    send_sem=sort_send.at[half],
                    recv_sem=sort_recv.at[j],
                    device_id={"blk": target, "cuts": cut},
                    device_id_type=MESH,
                ).start()
                return carry

            lax.fori_loop(1, groups, one, 0)
            pick(0)
            pltpu.make_async_copy(leave[half].at[0, pl.ds(first, count)], place, sort_recv.at[j]).start()

        if first == 0 and quarter + 1 < QUARTERS:
            spread(quarter + 1)

    def along(j, owner, target, arrival, side=None):
        columns = pl.ds(0, span) if side is None else pl.ds(side * (span // 2), span // 2)
        view = rows[j].at[:, pl.ds(pl.multiple_of(owner * 16, 16), 16), columns]
        return pltpu.make_async_remote_copy(
            src_ref=view,
            dst_ref=view,
            send_sem=way_sem.at[j],
            recv_sem=arrival.at[j],
            device_id={"blk": group, "cuts": target},
            device_id_type=MESH,
        )

    def piece(j, side=False):
        return rows[j].at[:, pl.ds(0, 16), pl.ds(0, span // (2 if side else 1))]

    def turn(j):
        wait_for(piece(j), sort_recv.at[j])
        along(j, cut, high, from_low).start()
        along(j, cut, low, from_high).start()
        along(j, cut, twin, from_twin).start()
        block_copy(j).start()

    def relay(j):
        wait_for(piece(j), from_low.at[j])
        along(j, low, high, from_low2, 0).start()
        along(j, low, twin, from_twin).start()
        wait_for(piece(j), from_high.at[j])
        along(j, high, low, from_high2, 1).start()
        along(j, high, twin, from_twin).start()

    def finish(j):
        wait_for(piece(j, True), from_low2.at[j])
        along(j, far, twin, from_twin, 0).start()
        wait_for(piece(j, True), from_high2.at[j])
        along(j, far, twin, from_twin, 1).start()

    def multiply(j):
        wait_for(rows[j].at[:, pl.ds(0, 64)], from_twin.at[j])
        block_copy(j).wait()
        product = jnp.dot(rows[j][0], blocks[j][0], preferred_element_type=jnp.float32)
        for block in range(1, chunks[j][2]):
            product += jnp.dot(rows[j][block], blocks[j][block], preferred_element_type=jnp.float32)
        product = product.reshape(total.shape)
        if j == 0:
            total[...] = product
        else:
            total[...] += product

    spread(0)
    for j in range(SORT_AHEAD):
        sort(j)
    for t in range(parts + 3):
        if t + SORT_AHEAD < parts:
            sort(t + SORT_AHEAD)
        if t < parts:
            turn(t)
        if 0 <= t - 1 < parts:
            relay(t - 1)
        if 0 <= t - 2 < parts:
            finish(t - 2)
        if 0 <= t - 3 < parts:
            multiply(t - 3)

    def scatter(offset, carry):
        target = moved(group, offset)
        pltpu.make_async_remote_copy(
            src_ref=total.at[target],
            dst_ref=sums.at[offset],
            send_sem=sum_send,
            recv_sem=sum_recv,
            device_id={"blk": target, "cuts": cut},
            device_id_type=MESH,
        ).start()
        return carry

    lax.fori_loop(1, groups, scatter, 0)
    line = lax.broadcasted_iota(jnp.int32, (8, width), 0)
    energy = jnp.zeros((8, width), jnp.float32)
    for i in range(8):
        pair = group * 8 + i
        energy = jnp.where(line == i, occ[pairs[0, pair]] + occ[pairs[1, pair]], energy)
    denominator = energy - ab[...].reshape(1, width)
    wait_for(sums.at[pl.ds(1, groups - 1)], sum_recv)
    ladder = total[group]
    for offset in range(1, groups):
        ladder = ladder + sums[offset]
    mine[...] = ladder / denominator

    def share(offset, carry):
        pltpu.make_async_remote_copy(
            src_ref=mine,
            dst_ref=out.at[group],
            send_sem=out_send,
            recv_sem=out_recv,
            device_id={"blk": moved(group, offset), "cuts": cut},
            device_id_type=MESH,
        ).start()
        return carry

    lax.fori_loop(1, groups, share, 0)
    keep = pltpu.make_async_copy(mine, out.at[group], end_sem)
    keep.start()
    for half in range(2):
        wait_for(middle[half].at[pl.ds(8, 120)], spread_send.at[half])
        wait_for(leave[half].at[pl.ds(1, groups - 1)], sort_send.at[half])
    for j in range(parts):
        wait_for(rows[j].at[:, pl.ds(0, 112)], way_sem.at[j])
    wait_for(sums.at[pl.ds(1, groups - 1)], sum_send)
    wait_for(sums.at[pl.ds(1, groups - 1)], out_recv)
    wait_for(sums.at[pl.ds(1, groups - 1)], out_send)
    keep.wait()


def on_device(integrals, amplitudes, tile_index, live_blocks, pair_index, occ_energy, ab_energy):
    groups = lax.axis_size("blk")
    per_group, depth, width = integrals.shape
    rows = amplitudes.shape[1]
    pairs = rows * lax.axis_size("cuts")
    part_rows = pairs // groups
    span = HUBS * LANES
    parts = len(CHUNKS)
    smem, vmem, hbm = (pl.BlockSpec(memory_space=space) for space in (pltpu.SMEM, pltpu.VMEM, pl.ANY))
    dma = pltpu.SemaphoreType.DMA
    scratch = [pltpu.VMEM(amplitudes.shape, jnp.bfloat16)]
    scratch += [pltpu.VMEM((groups, part_rows, width), jnp.float32)] * 2
    scratch += [pltpu.VMEM((part_rows, width), jnp.float32)]
    scratch += [pltpu.VMEM((groups * per_group, rows, LANES), jnp.bfloat16)] * 2
    scratch += [pltpu.VMEM((groups, per_group, rows, LANES), jnp.bfloat16)] * 2
    scratch += [pltpu.VMEM((count, span, width), jnp.bfloat16) for _, _, count in CHUNKS]
    scratch += [pltpu.VMEM((count, pairs, span), jnp.bfloat16) for _, _, count in CHUNKS]
    scratch += [dma, dma((parts,)), dma((2,)), dma((2,)), dma((2,)), dma((parts,))] + [dma((parts,))] * 6 + [dma] * 5
    update = pl.pallas_call(
        functools.partial(kernel, CHUNKS),
        out_shape=pltpu.VMEM((groups, part_rows, width), jnp.float32),
        in_specs=[smem, smem, smem, smem, vmem, hbm, hbm],
        out_specs=vmem,
        scratch_shapes=scratch,
        compiler_params=pltpu.CompilerParams(collective_id=0, has_side_effects=True, vmem_limit_bytes=56 << 20),
        cost_estimate=pl.CostEstimate(flops=2 * pairs * per_group * depth * width, bytes_accessed=integrals.size * 2, transcendentals=0),
        name="ladder",
    )(tile_index, live_blocks, pair_index.T, occ_energy, ab_energy, integrals, amplitudes)
    return update.reshape(pairs, width)


def solution(mesh):
    in_specs = (P("blk", None, "cuts"), P("blk", "cuts", None), P(), P(), P(), P(), P("cuts"))
    out_specs = P(None, "cuts")
    return jax.shard_map(
        on_device, mesh=mesh, in_specs=in_specs, out_specs=out_specs, check_vma=False
    )
```

time: 80.4 us -> 73.6 us (0.915)
  Pallas kernels: 77.9 us -> 72.8 us
  local copies, waits for them, and re-layouts: 1.62 us -> 0.68 us
    pallas_call x1, Pallas kernels: 77.9 us -> 72.8 us  [on_device(): pl.pallas_call(functools.partial(kernel, CHUNKS), out_shape=pltpu.VMEM((g...]
    unnamed x1, local copies, waits for them, and re-layouts: 1.62 us -> 0.68 us
where the time goes in v4:
time: 73.6 us; the launch traced here: 73.5 us
  Pallas kernels  72.8 us (99%)
    pallas_call x1, Pallas kernels, on_device(): pl.pallas_call(functools.partial(kernel, CHUNKS), out_shape=pltpu.VMEM((g...  72.8 us

profile of v4, /device:TPU:0, one launch (start us, length us, event | category | flops | bytes accessed | tf_op | source)
XLA Modules:
  0.0 73.5 jit_solution(8401701118138987637)
XLA Ops:
  0.0 72.8 %ladder.1 = f32[16,8,384]{2,1,0:T(8,128)S(1)} custom-call(s32[128]{0:T(128)} %refs_0_.1, s32[16]{0:T(128)} %refs_1_.1, s32[2,128]{1,0:T(2,128)} %bitcast.3, f32[160]{0:T(256)} %refs_3_.1, f32[384]{0:T(512)} %refs_4_.1, bf16[8,4096,384]{2,1,0:T(8,128)(2,1)} %refs_5_.1, bf16[8,16,4096]{2,1,0:T(8,128)(2,1)} %refs_6_.1), custom_call_target="tpu_custom_call" | custom-call | flops 3221225472 | bytes 25165824 | tf_op jit(solution)/shard_map/ladder/pallas_call | solution.py:268
  72.8 0.7 copy.9

commit v5 on v4

--- a/solution.py
+++ b/solution.py
@@ -11,7 +11,11 @@
 QUARTERS = 4
 HUBS = 8
 CHUNKS = tuple((quarter, first, 4) for quarter in range(QUARTERS) for first in range(0, 8, 4))
-SORT_AHEAD = 2
+BANDS = ((0, 256), (256, 128))
+TAIL = (2, 2)
+PIECES = tuple((j, 0, chunk[2]) for j, chunk in enumerate(CHUNKS[:-1])) + tuple(
+    (len(CHUNKS) - 1, sum(TAIL[:i]), size) for i, size in enumerate(TAIL)
+)
 STRIDE = 5
 MESH = pl.DeviceIdType.MESH
 
@@ -134,116 +138,152 @@
         if first == 0 and quarter + 1 < QUARTERS:
             spread(quarter + 1)
 
-    def along(j, owner, target, arrival, side=None):
+    def along(u, owner, target, arrival, side=None):
+        j, first, count = PIECES[u]
         columns = pl.ds(0, span) if side is None else pl.ds(side * (span // 2), span // 2)
-        view = rows[j].at[:, pl.ds(pl.multiple_of(owner * 16, 16), 16), columns]
+        view = rows[j].at[pl.ds(first, count), pl.ds(pl.multiple_of(owner * 16, 16), 16), columns]
         return pltpu.make_async_remote_copy(
             src_ref=view,
             dst_ref=view,
-            send_sem=way_sem.at[j],
-            recv_sem=arrival.at[j],
+            send_sem=way_sem.at[u],
+            recv_sem=arrival.at[u],
             device_id={"blk": group, "cuts": target},
             device_id_type=MESH,
         )
 
-    def piece(j, side=False):
-        return rows[j].at[:, pl.ds(0, 16), pl.ds(0, span // (2 if side else 1))]
-
-    def turn(j):
-        wait_for(piece(j), sort_recv.at[j])
-        along(j, cut, high, from_low).start()
-        along(j, cut, low, from_high).start()
-        along(j, cut, twin, from_twin).start()
-        block_copy(j).start()
-
-    def relay(j):
-        wait_for(piece(j), from_low.at[j])
-        along(j, low, high, from_low2, 0).start()
-        along(j, low, twin, from_twin).start()
-        wait_for(piece(j), from_high.at[j])
-        along(j, high, low, from_high2, 1).start()
-        along(j, high, twin, from_twin).start()
-
-    def finish(j):
-        wait_for(piece(j, True), from_low2.at[j])
-        along(j, far, twin, from_twin, 0).start()
-        wait_for(piece(j, True), from_high2.at[j])
-        along(j, far, twin, from_twin, 1).start()
-
-    def multiply(j):
-        wait_for(rows[j].at[:, pl.ds(0, 64)], from_twin.at[j])
-        block_copy(j).wait()
-        product = jnp.dot(rows[j][0], blocks[j][0], preferred_element_type=jnp.float32)
-        for block in range(1, chunks[j][2]):
-            product += jnp.dot(rows[j][block], blocks[j][block], preferred_element_type=jnp.float32)
-        product = product.reshape(total.shape)
-        if j == 0:
-            total[...] = product
+    def piece(u, lines=16, columns=span):
+        j, first, count = PIECES[u]
+        return rows[j].at[pl.ds(first, count), pl.ds(0, lines), pl.ds(0, columns)]
+
+    def turn(u):
+        j, first, _ = PIECES[u]
+        if first == 0:
+            wait_for(rows[j].at[:, pl.ds(0, 16)], sort_recv.at[j])
+        along(u, cut, high, from_low).start()
+        along(u, cut, low, from_high).start()
+        along(u, cut, twin, from_twin).start()
+        if first == 0:
+            block_copy(j).start()
+
+    def relay(u):
+        wait_for(piece(u), from_low.at[u])
+        along(u, low, high, from_low2, 0).start()
+        along(u, low, twin, from_twin).start()
+        wait_for(piece(u), from_high.at[u])
+        along(u, high, low, from_high2, 1).start()
+        along(u, high, twin, from_twin).start()
+
+    def finish(u):
+        wait_for(piece(u, 16, span // 2), from_low2.at[u])
+        along(u, far, twin, from_twin, 0).start()
+        wait_for(piece(u, 16, span // 2), from_high2.at[u])
+        along(u, far, twin, from_twin, 1).start()
+
+    def multiply(u):
+        j, first, count = PIECES[u]
+        wait_for(piece(u, 64), from_twin.at[u])
+        if first == 0:
+            block_copy(j).wait()
+        for band in range(len(BANDS)) if u == len(PIECES) - 1 else (None,):
+            columns = slice(None) if band is None else pl.ds(*BANDS[band])
+            product = jnp.dot(rows[j][first], blocks[j][first, :, columns], preferred_element_type=jnp.float32)
+            for block in range(first + 1, first + count):
+                product += jnp.dot(rows[j][block], blocks[j][block, :, columns], preferred_element_type=jnp.float32)
+            product = product.reshape(groups, 8, product.shape[1])
+            if u == 0:
+                total[:, :, columns] = product
+            else:
+                total[:, :, columns] += product
+            if band is not None:
+                scatter(band)
+
+    def scatter(band):
+        columns = pl.ds(*BANDS[band])
+
+        def one(step, carry):
+            offset = (step * STRIDE) & 15
+            target = moved(group, offset)
+            pltpu.make_async_remote_copy(
+                src_ref=total.at[target, :, columns],
+                dst_ref=sums.at[offset, :, columns],
+                send_sem=sum_send.at[band],
+                recv_sem=sum_recv.at[band],
+                device_id={"blk": target, "cuts": cut},
+                device_id_type=MESH,
+            ).start()
+            return carry
+
+        lax.fori_loop(1, groups, one, 0)
+
+    spread(0)
+    sort(0)
+    for t in range(parts):
+        if t + 1 < parts:
+            sort(t + 1)
+            turn(t)
         else:
-            total[...] += product
-
-    spread(0)
-    for j in range(SORT_AHEAD):
-        sort(j)
-    for t in range(parts + 3):
-        if t + SORT_AHEAD < parts:
-            sort(t + SORT_AHEAD)
-        if t < parts:
-            turn(t)
-        if 0 <= t - 1 < parts:
+            for u in range(t, len(PIECES)):
+                turn(u)
+        if t >= 1:
             relay(t - 1)
-        if 0 <= t - 2 < parts:
+        if t >= 3:
+            multiply(t - 3)
+        if t >= 2:
             finish(t - 2)
-        if 0 <= t - 3 < parts:
-            multiply(t - 3)
-
-    def scatter(offset, carry):
-        target = moved(group, offset)
-        pltpu.make_async_remote_copy(
-            src_ref=total.at[target],
-            dst_ref=sums.at[offset],
-            send_sem=sum_send,
-            recv_sem=sum_recv,
-            device_id={"blk": target, "cuts": cut},
-            device_id_type=MESH,
-        ).start()
-        return carry
-
-    lax.fori_loop(1, groups, scatter, 0)
+    last = range(parts - 1, len(PIECES))
+    for u in last:
+        relay(u)
+    multiply(parts - 3)
+    finish(parts - 2)
+    for u in last:
+        finish(u)
+    for u in range(parts - 2, len(PIECES)):
+        multiply(u)
+
     line = lax.broadcasted_iota(jnp.int32, (8, width), 0)
     energy = jnp.zeros((8, width), jnp.float32)
     for i in range(8):
         pair = group * 8 + i
         energy = jnp.where(line == i, occ[pairs[0, pair]] + occ[pairs[1, pair]], energy)
     denominator = energy - ab[...].reshape(1, width)
-    wait_for(sums.at[pl.ds(1, groups - 1)], sum_recv)
-    ladder = total[group]
-    for offset in range(1, groups):
-        ladder = ladder + sums[offset]
-    mine[...] = ladder / denominator
-
-    def share(offset, carry):
-        pltpu.make_async_remote_copy(
-            src_ref=mine,
-            dst_ref=out.at[group],
-            send_sem=out_send,
-            recv_sem=out_recv,
-            device_id={"blk": moved(group, offset), "cuts": cut},
-            device_id_type=MESH,
-        ).start()
-        return carry
-
-    lax.fori_loop(1, groups, share, 0)
+
+    def others(band):
+        return sums.at[pl.ds(1, groups - 1), :, pl.ds(*BANDS[band])]
+
+    def share(band):
+        columns = pl.ds(*BANDS[band])
+        wait_for(others(band), sum_recv.at[band])
+        ladder = total[group, :, columns]
+        for offset in range(1, groups):
+            ladder = ladder + sums[offset, :, columns]
+        mine[:, columns] = ladder / denominator[:, BANDS[band][0]:sum(BANDS[band])]
+
+        def one(step, carry):
+            pltpu.make_async_remote_copy(
+                src_ref=mine.at[:, columns],
+                dst_ref=out.at[group, :, columns],
+                send_sem=out_send.at[band],
+                recv_sem=out_recv.at[band],
+                device_id={"blk": moved(group, (step * STRIDE) & 15), "cuts": cut},
+                device_id_type=MESH,
+            ).start()
+            return carry
+
+        lax.fori_loop(1, groups, one, 0)
+
+    for band in range(len(BANDS)):
+        share(band)
     keep = pltpu.make_async_copy(mine, out.at[group], end_sem)
     keep.start()
     for half in range(2):
         wait_for(middle[half].at[pl.ds(8, 120)], spread_send.at[half])
         wait_for(leave[half].at[pl.ds(1, groups - 1)], sort_send.at[half])
-    for j in range(parts):
-        wait_for(rows[j].at[:, pl.ds(0, 112)], way_sem.at[j])
-    wait_for(sums.at[pl.ds(1, groups - 1)], sum_send)
-    wait_for(sums.at[pl.ds(1, groups - 1)], out_recv)
-    wait_for(sums.at[pl.ds(1, groups - 1)], out_send)
+    for u in range(len(PIECES)):
+        wait_for(piece(u, 112), way_sem.at[u])
+    for band in range(len(BANDS)):
+        wait_for(others(band), sum_send.at[band])
+        wait_for(others(band), out_recv.at[band])
+        wait_for(others(band), out_send.at[band])
     keep.wait()
 
 
@@ -264,7 +304,7 @@
     scratch += [pltpu.VMEM((groups, per_group, rows, LANES), jnp.bfloat16)] * 2
     scratch += [pltpu.VMEM((count, span, width), jnp.bfloat16) for _, _, count in CHUNKS]
     scratch += [pltpu.VMEM((count, pairs, span), jnp.bfloat16) for _, _, count in CHUNKS]
-    scratch += [dma, dma((parts,)), dma((2,)), dma((2,)), dma((2,)), dma((parts,))] + [dma((parts,))] * 6 + [dma] * 5
+    scratch += [dma, dma((parts,)), dma((2,)), dma((2,)), dma((2,)), dma((parts,))] + [dma((len(PIECES),))] * 6 + [dma((len(BANDS),))] * 4 + [dma]
     update = pl.pallas_call(
         functools.partial(kernel, CHUNKS),
         out_shape=pltpu.VMEM((groups, part_rows, width), jnp.float32),

time: 73.6 us -> 71.8 us (0.976)
  Pallas kernels: 72.8 us -> 71 us
    pallas_call x1, Pallas kernels: 72.8 us -> 71 us  [on_device(): pl.pallas_call(functools.partial(kernel, CHUNKS), out_shape=pltpu.VMEM((g...]
where the time goes in v5:
time: 71.8 us; the launch traced here: 71.6 us
  Pallas kernels  71 us (99%)
    pallas_call x1, Pallas kernels, on_device(): pl.pallas_call(functools.partial(kernel, CHUNKS), out_shape=pltpu.VMEM((g...  71 us

profile of v5, /device:TPU:0, one launch (start us, length us, event | category | flops | bytes accessed | tf_op | source)
XLA Modules:
  0.0 71.6 jit_solution(11035461792762434054)
XLA Ops:
  0.0 71.0 %ladder.1 = f32[16,8,384]{2,1,0:T(8,128)S(1)} custom-call(s32[128]{0:T(128)} %refs_0_.1, s32[16]{0:T(128)} %refs_1_.1, s32[2,128]{1,0:T(2,128)} %bitcast.3, f32[160]{0:T(256)} %refs_3_.1, f32[384]{0:T(512)} %refs_4_.1, bf16[8,4096,384]{2,1,0:T(8,128)(2,1)} %refs_5_.1, bf16[8,16,4096]{2,1,0:T(8,128)(2,1)} %refs_6_.1), custom_call_target="tpu_custom_call" | custom-call | flops 3221225472 | bytes 25165824 | tf_op jit(solution)/shard_map/ladder/pallas_call | solution.py:308
  71.0 0.7 copy.9

commit v6 on v5

--- a/solution.py
+++ b/solution.py
@@ -16,7 +16,7 @@
 PIECES = tuple((j, 0, chunk[2]) for j, chunk in enumerate(CHUNKS[:-1])) + tuple(
     (len(CHUNKS) - 1, sum(TAIL[:i]), size) for i, size in enumerate(TAIL)
 )
-STRIDE = 5
+FAR_FIRST = (10, 6, 9, 11, 14, 2, 8, 5, 7, 13, 15, 1, 3, 4, 12)
 MESH = pl.DeviceIdType.MESH
 
 
@@ -118,8 +118,7 @@
                     leave[half][offset, block] = jnp.where(live > block, tile, jnp.zeros_like(tile))
                 return target
 
-            def one(step, carry):
-                offset = (step * STRIDE) & 15
+            def one(offset):
                 target = pick(offset)
                 pltpu.make_async_remote_copy(
                     src_ref=leave[half].at[offset, pl.ds(first, count)],
@@ -129,9 +128,9 @@
                     device_id={"blk": target, "cuts": cut},
                     device_id_type=MESH,
                 ).start()
-                return carry
-
-            lax.fori_loop(1, groups, one, 0)
+
+            for offset in FAR_FIRST:
+                one(offset)
             pick(0)
             pltpu.make_async_copy(leave[half].at[0, pl.ds(first, count)], place, sort_recv.at[j]).start()
 
@@ -200,8 +199,7 @@
     def scatter(band):
         columns = pl.ds(*BANDS[band])
 
-        def one(step, carry):
-            offset = (step * STRIDE) & 15
+        def one(offset):
             target = moved(group, offset)
             pltpu.make_async_remote_copy(
                 src_ref=total.at[target, :, columns],
@@ -211,9 +209,9 @@
                 device_id={"blk": target, "cuts": cut},
                 device_id_type=MESH,
             ).start()
-            return carry
-
-        lax.fori_loop(1, groups, one, 0)
+
+        for offset in FAR_FIRST:
+            one(offset)
 
     spread(0)
     sort(0)
@@ -258,18 +256,18 @@
             ladder = ladder + sums[offset, :, columns]
         mine[:, columns] = ladder / denominator[:, BANDS[band][0]:sum(BANDS[band])]
 
-        def one(step, carry):
+        def one(offset):
             pltpu.make_async_remote_copy(
                 src_ref=mine.at[:, columns],
                 dst_ref=out.at[group, :, columns],
                 send_sem=out_send.at[band],
                 recv_sem=out_recv.at[band],
-                device_id={"blk": moved(group, (step * STRIDE) & 15), "cuts": cut},
+                device_id={"blk": moved(group, offset), "cuts": cut},
                 device_id_type=MESH,
             ).start()
-            return carry
-
-        lax.fori_loop(1, groups, one, 0)
+
+        for offset in FAR_FIRST:
+            one(offset)
 
     for band in range(len(BANDS)):
         share(band)

time: 71.8 us -> 71 us (0.989)
  Pallas kernels: 71 us -> 70.2 us
    pallas_call x1, Pallas kernels: 71 us -> 70.2 us  [on_device(): pl.pallas_call(functools.partial(kernel, CHUNKS), out_shape=pltpu.VMEM((g...]
where the time goes in v6:
time: 71 us; the launch traced here: 70.9 us
  Pallas kernels  70.2 us (99%)
    pallas_call x1, Pallas kernels, on_device(): pl.pallas_call(functools.partial(kernel, CHUNKS), out_shape=pltpu.VMEM((g...  70.2 us

profile of v6, /device:TPU:0, one launch (start us, length us, event | category | flops | bytes accessed | tf_op | source)
XLA Modules:
  0.0 70.9 jit_solution(15785167876840240278)
XLA Ops:
  0.0 70.2 %ladder.1 = f32[16,8,384]{2,1,0:T(8,128)S(1)} custom-call(s32[128]{0:T(128)} %refs_0_.1, s32[16]{0:T(128)} %refs_1_.1, s32[2,128]{1,0:T(2,128)} %bitcast.3, f32[160]{0:T(256)} %refs_3_.1, f32[384]{0:T(512)} %refs_4_.1, bf16[8,4096,384]{2,1,0:T(8,128)(2,1)} %refs_5_.1, bf16[8,16,4096]{2,1,0:T(8,128)(2,1)} %refs_6_.1), custom_call_target="tpu_custom_call" | custom-call | flops 3221225472 | bytes 25165824 | tf_op jit(solution)/shard_map/ladder/pallas_call | solution.py:306
  70.2 0.7 copy.9

commit v7 on v6

--- a/solution.py
+++ b/solution.py
@@ -44,11 +44,11 @@
 
     barrier = pltpu.get_barrier_semaphore()
 
-    def greet(offset, carry):
+    def greet(offset):
         pl.semaphore_signal(barrier, inc=1, device_id={"blk": moved(group, offset), "cuts": cut}, device_id_type=MESH)
-        return carry
-
-    lax.fori_loop(1, groups, greet, 0)
+
+    for offset in FAR_FIRST:
+        greet(offset)
     for other in (high, low, twin):
         pl.semaphore_signal(barrier, inc=1, device_id={"blk": group, "cuts": other}, device_id_type=MESH)
     pl.semaphore_wait(barrier, groups - 1 + 3)

time: 71 us -> 70.6 us (level)
  no operation moved by 1% of the time
where the time goes in v7:
time: 70.6 us; the launch traced here: 70.5 us
  Pallas kernels  69.8 us (99%)
    pallas_call x1, Pallas kernels, on_device(): pl.pallas_call(functools.partial(kernel, CHUNKS), out_shape=pltpu.VMEM((g...  69.8 us

profile of v7, /device:TPU:0, one launch (start us, length us, event | category | flops | bytes accessed | tf_op | source)
XLA Modules:
  0.0 70.5 jit_solution(15764666465569138814)
XLA Ops:
  0.0 69.8 %ladder.1 = f32[16,8,384]{2,1,0:T(8,128)S(1)} custom-call(s32[128]{0:T(128)} %refs_0_.1, s32[16]{0:T(128)} %refs_1_.1, s32[2,128]{1,0:T(2,128)} %bitcast.3, f32[160]{0:T(256)} %refs_3_.1, f32[384]{0:T(512)} %refs_4_.1, bf16[8,4096,384]{2,1,0:T(8,128)(2,1)} %refs_5_.1, bf16[8,16,4096]{2,1,0:T(8,128)(2,1)} %refs_6_.1), custom_call_target="tpu_custom_call" | custom-call | flops 3221225472 | bytes 25165824 | tf_op jit(solution)/shard_map/ladder/pallas_call | solution.py:306
  69.8 0.7 copy.9
